TPU v7x, 32 devices: a whole 2x2x4 slice. The times are simulated.
32 devices in a mesh: space: 8 (over z, x), snap: 4 (over y, core).
Axes of the slice: x: 2, y: 2, z: 4, core: 2. Of those that a mesh axis runs over, the one named last changes fastest.
Arguments:
- velocity: bfloat16 [64, 3, 64, 32, 128], P('snap', None, 'space'), may hold values from -40 to 40
- phase_bins: int32 [64], replicated, may hold values from 0 to 23, as said below
- tile_owner: int32 [8], replicated, may hold values from 0 to 7, each once
Outputs:
- gram_tiles: float32 [8, 8, 64], P('space', None, 'snap')
Inputs may be any that keep to these rules, and one draw needn't show every extreme that they name: `phase_bins`: every bin holds at least one snapshot. `tile_owner`: each tile has exactly one owner.
All inputs are finite; a program needn't handle non-finite values.
Results may differ from a plain program's by a relative error of at most 0.0003.
Values may be sent and summed in bfloat16 or wider, within the bound.
A program may use at most 128 MiB of HBM per device.

v0:
```python
import functools
import jax
import jax.numpy as jnp
from jax import lax
from jax.experimental import pallas as pl
from jax.experimental.pallas import tpu as pltpu
from jax.sharding import PartitionSpec as P

NB = 24
MESH = pl.DeviceIdType.MESH
F32 = jnp.float32
BF16 = jnp.bfloat16
HIGH = lax.Precision.HIGHEST


def iota2(shape, dim):
    return lax.broadcasted_iota(jnp.int32, shape, dim)


def stencil(step):
    plus = jnp.where(step == 1, 8.0, 0.0) - jnp.where(step == 2, 1.0, 0.0)
    minus = jnp.where(step == -1, 8.0, 0.0) - jnp.where(step == -2, 1.0, 0.0)
    return plus - minus


def kernel(
    n_space, n_snap, inv_voxels,
    owner_ref, bins_ref, vel_ref, out_ref,
    ext, uu, perm, band_y, band_z, omega, send, recv, mean_mat, gram, mail, rows_in, cols_out, cols_in,
    local_sem, halo_send, halo_recv, a2a_send, a2a_recv, row_send, row_recv, col_send, col_recv,
):
    snaps, _, nx, ny, nz = vel_ref.shape
    total = snaps * n_snap
    half = snaps * ny // 2
    rows = snaps * ny
    part = rows // n_snap
    y_part = ny // n_snap
    pairs = nx // 2
    tile_rows = total // n_space
    chunks = 3 * pairs
    si = lax.axis_index("space")
    ti = lax.axis_index("snap")

    load_vw = pltpu.make_async_copy(vel_ref.at[:, 1:3], ext.at[:, :, 2 : nx + 2], local_sem.at[0])
    load_u = pltpu.make_async_copy(vel_ref.at[:, 0], uu, local_sem.at[1])
    load_vw.start()
    load_u.start()

    barrier = pltpu.get_barrier_semaphore()
    for o in range(1, n_snap):
        pl.semaphore_signal(
            barrier, inc=1, device_id={"snap": lax.rem(ti + o, n_snap)}, device_id_type=MESH
        )
    for o in range(1, n_space):
        pl.semaphore_signal(
            barrier, inc=1, device_id={"space": lax.rem(si + o, n_space)}, device_id_type=MESH
        )

    r = iota2((rows, rows), 0)
    c = iota2((rows, rows), 1)
    perm[...] = jnp.where(c == (r % snaps) * ny + r // snaps, 1.0, 0.0).astype(BF16)
    r = iota2((half, half), 0)
    c = iota2((half, half), 1)
    band_y[...] = jnp.where(r // ny == c // ny, stencil(c - r), 0.0).astype(BF16)
    r = iota2((2 * nz, 2 * nz), 0)
    c = iota2((2 * nz, 2 * nz), 1)
    band_z[...] = jnp.where(r // nz == c // nz, stencil(r - c), 0.0).astype(BF16)

    onehot = jnp.where(bins_ref[...] == iota2((32, total), 0), 1.0, 0.0).astype(F32)
    same = lax.dot_general(
        onehot, onehot, (((0,), (0,)), ((), ())), preferred_element_type=F32
    )
    averaging = same / jnp.sum(same, axis=0, keepdims=True)
    mean_mat[...] = averaging.astype(BF16)
    gram[...] = jnp.zeros_like(gram)

    pl.semaphore_wait(barrier, n_snap + n_space - 2)

    def to_left():
        return pltpu.make_async_remote_copy(
            vel_ref.at[:, 1:3, 0:2], ext.at[:, :, nx + 2 : nx + 4],
            halo_send.at[0], halo_recv.at[0],
            device_id={"space": si - 1}, device_id_type=MESH,
        )

    def to_right():
        return pltpu.make_async_remote_copy(
            vel_ref.at[:, 1:3, nx - 2 : nx], ext.at[:, :, 0:2],
            halo_send.at[1], halo_recv.at[1],
            device_id={"space": si + 1}, device_id_type=MESH,
        )

    @pl.when(si > 0)
    def _():
        to_left().start()

    @pl.when(si < n_space - 1)
    def _():
        to_right().start()

    @pl.when(si == 0)
    def _():
        ext[:, :, 0:2] = jnp.zeros((snaps, 2, 2, ny, nz), BF16)

    @pl.when(si == n_space - 1)
    def _():
        ext[:, :, nx + 2 : nx + 4] = jnp.zeros((snaps, 2, 2, ny, nz), BF16)

    order = sorted(range(1, n_snap), key=lambda o: abs(o - n_snap // 2))

    def a2a(k, o):
        dst = lax.rem(ti + o, n_snap)
        return pltpu.make_async_remote_copy(
            send.at[k, pl.ds(pl.multiple_of(dst * part, part), part)],
            recv.at[k, ti],
            a2a_send.at[k, o - 1], a2a_recv.at[k, o - 1],
            device_id={"snap": dst}, device_id_type=MESH,
        )

    def ship(k):
        moved = jnp.dot(perm[...], omega[...], preferred_element_type=F32)
        send[k] = moved.astype(BF16)
        for o in order:
            a2a(k, o).start()
        recv[k, ti] = send[k, pl.ds(pl.multiple_of(ti * part, part), part)]

    h_snaps = snaps // 2

    def pair_vw(comp, x, h):
        s = slice(h * h_snaps, (h + 1) * h_snaps)
        return jnp.concatenate(
            [ext[s, comp, x + 2 + i].reshape(half, nz) for i in range(2)], axis=1
        )

    def pair_u(x, h):
        s = slice(h * h_snaps, (h + 1) * h_snaps)
        return jnp.concatenate([uu[s, x + i].reshape(half, nz) for i in range(2)], axis=1)

    def d1_pair(comp, x, h):
        s = slice(h * h_snaps, (h + 1) * h_snaps)
        f = [ext[s, comp, x + i].reshape(half, nz).astype(F32) for i in range(6)]
        return jnp.concatenate(
            [8.0 * (f[i + 3] - f[i + 1]) - (f[i + 4] - f[i]) for i in range(2)], axis=1
        )

    def d2(field):
        return jnp.dot(band_y[...], field, preferred_element_type=F32)

    def d3(field):
        return jnp.dot(field, band_z[...], preferred_element_type=F32)

    def put(h, value):
        omega[h * half : (h + 1) * half] = (value * (1.0 / 12.0)).astype(BF16)

    load_vw.wait()

    def first_component(p, _):
        for h in range(2):
            put(h, d2(pair_vw(1, 2 * p, h)) - d3(pair_vw(0, 2 * p, h)))
        ship(p)
        return 0

    lax.fori_loop(0, pairs, first_component, 0)
    load_u.wait()

    def other_components(k, x):
        for h in range(2):
            put(h, d3(pair_u(x, h)) - d1_pair(1, x, h))
        ship(k)
        for h in range(2):
            put(h, d1_pair(0, x, h) - d2(pair_u(x, h)))
        ship(k + 1)

    def inner(p, _):
        other_components(pairs + 2 * p, 2 * p + 2)
        return 0

    lax.fori_loop(0, pairs - 2, inner, 0)

    @pl.when(si < n_space - 1)
    def _():
        to_left().wait_recv()

    @pl.when(si > 0)
    def _():
        to_right().wait_recv()

    def outer(p, _):
        other_components(chunks - 4 + 2 * p, p * (nx - 2))
        return 0

    lax.fori_loop(0, 2, outer, 0)

    def accumulate(k, _):
        for o in order:
            a2a(k, o).wait_recv()
        columns = jnp.concatenate(
            [
                jnp.concatenate(
                    [recv[k, t, y * snaps : (y + 1) * snaps] for t in range(n_snap)], axis=0
                )
                for y in range(y_part)
            ],
            axis=1,
        )
        mean = jnp.dot(mean_mat[...], columns, preferred_element_type=F32)
        near = (columns.astype(F32) - mean).astype(BF16)
        gram[...] += lax.dot_general(
            near, near, (((1,), (1,)), ((), ())), preferred_element_type=F32
        )
        return 0

    lax.fori_loop(0, chunks, accumulate, 0)

    eye = jnp.where(iota2((total, total), 0) == iota2((total, total), 1), 1.0, 0.0)
    onehot = jnp.where(bins_ref[...] == iota2((32, total), 0), 1.0, 0.0).astype(F32)
    same = lax.dot_general(
        onehot, onehot, (((0,), (0,)), ((), ())), preferred_element_type=F32
    )
    centre = eye - same / jnp.sum(same, axis=0, keepdims=True)
    r = iota2((total, total), 0)
    c = iota2((total, total), 1)
    owners = jnp.zeros((total, total), jnp.int32)
    for t in range(n_space):
        owners = jnp.where(c // tile_rows == t, owner_ref[t], owners)
    place = jnp.where((r // tile_rows == owners) & (r % tile_rows == c % tile_rows), 1.0, 0.0)
    lines = jnp.dot(
        jnp.dot(place, centre, preferred_element_type=F32, precision=HIGH),
        gram[...], preferred_element_type=F32, precision=HIGH,
    )
    done = jnp.dot(lines, centre, preferred_element_type=F32, precision=HIGH) * inv_voxels
    mail[...] = jnp.zeros_like(mail)
    mail[:, 0:total] = done

    def row_copy(o):
        dst = lax.rem(si + o, n_space)
        return pltpu.make_async_remote_copy(
            mail.at[pl.ds(pl.multiple_of(dst * tile_rows, tile_rows), tile_rows)],
            rows_in.at[si], row_send.at[o - 1], row_recv.at[o - 1],
            device_id={"space": dst}, device_id_type=MESH,
        )

    for o in range(1, n_space):
        row_copy(o).start()
    rows_in[si] = mail[pl.ds(pl.multiple_of(si * tile_rows, tile_rows), tile_rows)]
    for o in range(1, n_space):
        row_copy(o).wait_recv()
    mine = jnp.sum(rows_in[...], axis=0)
    cols_out[...] = mine

    def col_copy(o):
        return pltpu.make_async_remote_copy(
            cols_out, cols_in.at[o - 1], col_send.at[o - 1], col_recv.at[o - 1],
            device_id={"snap": lax.rem(ti + o, n_snap)}, device_id_type=MESH,
        )

    for o in order:
        col_copy(o).start()
    for o in order:
        col_copy(o).wait_recv()
    out_ref[...] = mine + jnp.sum(cols_in[...], axis=0)

    def drain(k, _):
        for o in order:
            a2a(k, o).wait_send()
        return 0

    lax.fori_loop(0, chunks, drain, 0)

    @pl.when(si > 0)
    def _():
        to_left().wait_send()

    @pl.when(si < n_space - 1)
    def _():
        to_right().wait_send()

    for o in range(1, n_space):
        row_copy(o).wait_send()
    for o in order:
        col_copy(o).wait_send()


def per_device(velocity, phase_bins, tile_owner):
    n_space = lax.axis_size("space")
    n_snap = lax.axis_size("snap")
    snaps, _, nx, ny, nz = velocity.shape
    total = snaps * n_snap
    rows = snaps * ny
    part = rows // n_snap
    chunks = 3 * (nx // 2)
    tile_rows = total // n_space
    wide = -(-total // 128) * 128
    dma = pltpu.SemaphoreType.DMA
    summed = pl.pallas_call(
        functools.partial(kernel, n_space, n_snap, 1.0 / (n_space * nx * ny * nz)),
        out_shape=jax.ShapeDtypeStruct((tile_rows, wide), F32),
        in_specs=[
            pl.BlockSpec(memory_space=pltpu.SMEM),
            pl.BlockSpec(memory_space=pltpu.VMEM),
            pl.BlockSpec(memory_space=pl.ANY),
        ],
        out_specs=pl.BlockSpec(memory_space=pltpu.VMEM),
        scratch_shapes=[
            pltpu.VMEM((snaps, 2, nx + 4, ny, nz), BF16),
            pltpu.VMEM((snaps, nx, ny, nz), BF16),
            pltpu.VMEM((rows, rows), BF16),
            pltpu.VMEM((rows // 2, rows // 2), BF16),
            pltpu.VMEM((2 * nz, 2 * nz), BF16),
            pltpu.VMEM((rows, 2 * nz), BF16),
            pltpu.VMEM((chunks, rows, 2 * nz), BF16),
            pltpu.VMEM((chunks, n_snap, part, 2 * nz), BF16),
            pltpu.VMEM((total, total), BF16),
            pltpu.VMEM((total, total), F32),
            pltpu.VMEM((total, wide), F32),
            pltpu.VMEM((n_space, tile_rows, wide), F32),
            pltpu.VMEM((tile_rows, wide), F32),
            pltpu.VMEM((n_snap - 1, tile_rows, wide), F32),
            dma((2,)),
            dma((2,)),
            dma((2,)),
            dma((chunks, n_snap - 1)),
            dma((chunks, n_snap - 1)),
            dma((n_space - 1,)),
            dma((n_space - 1,)),
            dma((n_snap - 1,)),
            dma((n_snap - 1,)),
        ],
        compiler_params=pltpu.CompilerParams(
            collective_id=0, has_side_effects=True, vmem_limit_bytes=48 * 1024 * 1024
        ),
        cost_estimate=pl.CostEstimate(
            flops=4_000_000_000, bytes_accessed=4_000_000, transcendentals=0
        ),
    )(tile_owner, phase_bins.reshape(1, total), velocity)
    return lax.dynamic_slice_in_dim(summed, lax.axis_index("snap") * snaps, snaps, axis=1)[None]


def solution(mesh):
    return jax.shard_map(
        per_device,
        mesh=mesh,
        in_specs=(P("snap", None, "space", None, None), P(), P()),
        out_specs=P("space", None, "snap"),
        check_vma=False,
    )
```

profile of v0, /device:TPU:0, one launch (start us, length us, event | category | flops | bytes accessed | tf_op | source)
XLA Modules:
  0.0 55.5 jit_solution(5615086263820355611)
XLA Ops:
  0.0 0.0 copy-start
  0.0 1.9 %copy-done = bf16[16,3,8,32,128]{4,3,2,1,0:T(8,128)(2,1)S(1)} copy-done((bf16[16,3,8,32,128]{4,3,2,1,0:T(8,128)(2,1)S(1)}, bf16[16,3,8,32,128]{4,3,2,1,0:T(8,128)(2,1)}, u32[]{:S(2)}) %copy-start) | copy-done | bytes 3145752
  1.9 0.0 copy-start.1
  1.9 0.7 %copy-done.1 = s32[8]{0:T(128)S(1)} copy-done((s32[8]{0:T(128)S(1)}, s32[8]{0:T(128)}, u32[]{:S(2)}) %copy-start.1) | copy-done | bytes 56
  2.5 0.0 copy-start.2
  2.5 0.7 %copy-done.2 = s32[64]{0:T(128)S(1)} copy-done((s32[64]{0:T(128)S(1)}, s32[64]{0:T(128)}, u32[]{:S(2)}) %copy-start.2) | copy-done | bytes 280
  3.2 51.6 %shard_map.37 = f32[8,128]{1,0:T(8,128)S(1)} custom-call(s32[8]{0:T(128)S(1)} %copy-done.1, s32[1,64]{1,0:T(1,128)S(1)} %bitcast.3, bf16[16,3,8,32,128]{4,3,2,1,0:T(8,128)(2,1)S(1)} %copy-done), custom_call_target="tpu_custom_call" | custom-call | flops 4000000000 | bytes 4000000 | tf_op jit(solution)/shard_map/pallas_call | solution.py:295
  54.9 0.7 %dynamic-slice_bitcast_fusion = f32[1,8,16]{2,1,0:T(8,128)} fusion(f32[8,128]{1,0:T(8,128)S(1)} %shard_map.37, s32[]{:T(128)S(6)} %select_n.3), kind=kLoop, calls=%fused_computation | loop fusion | bytes 1028 | tf_op jit(solution)/shard_map/broadcast_in_dim | solution.py:336
Async XLA Ops:
  0.0 1.9 %copy-start = (bf16[16,3,8,32,128]{4,3,2,1,0:T(8,128)(2,1)S(1)}, bf16[16,3,8,32,128]{4,3,2,1,0:T(8,128)(2,1)}, u32[]{:S(2)}) copy-start(bf16[16,3,8,32,128]{4,3,2,1,0:T(8,128)(2,1)} %vel_ref.1) | copy-start | bytes 9437188
  1.9 0.7 %copy-start.1 = (s32[8]{0:T(128)S(1)}, s32[8]{0:T(128)}, u32[]{:S(2)}) copy-start(s32[8]{0:T(128)} %owner_ref.1) | copy-start | bytes 100
  2.5 0.7 %copy-start.2 = (s32[64]{0:T(128)S(1)}, s32[64]{0:T(128)}, u32[]{:S(2)}) copy-start(s32[64]{0:T(128)} %param.4) | copy-start | bytes 772
where the time goes:
time: 55.7 us; the launch traced here: 55.5 us
  Pallas kernels  51.6 us (93%)
  local copies, waits for them, and re-layouts  3.87 us (7%)
    pallas_call x1, Pallas kernels, per_device(): pl.pallas_call(functools.partial(kernel, n_space, n_snap, 1.0 / (n_space...  51.6 us
    unnamed x6, local copies, waits for them, and re-layouts  3.2 us

commit v1 on v0

v1 whole, which is shorter than its diff:
```python
import functools
import jax
import jax.numpy as jnp
from jax import lax
from jax.experimental import pallas as pl
from jax.experimental.pallas import tpu as pltpu
from jax.sharding import PartitionSpec as P

NB = 24
MESH = pl.DeviceIdType.MESH
F32 = jnp.float32
BF16 = jnp.bfloat16
HIGH = lax.Precision.HIGHEST


def iota2(shape, dim):
    return lax.broadcasted_iota(jnp.int32, shape, dim)


def stencil(step):
    plus = jnp.where(step == 1, 8.0, 0.0) - jnp.where(step == 2, 1.0, 0.0)
    minus = jnp.where(step == -1, 8.0, 0.0) - jnp.where(step == -2, 1.0, 0.0)
    return plus - minus


def kernel(
    n_space, n_snap, inv_voxels,
    owner_hbm, bins_hbm, vel_ref, out_ref,
    owner_ref, bins_ref, ext, uu, perm, band_y, band_z, omega, send, recv, mean_mat, centre_mat, left_mat, gram, mail, rows_in, cols_out, cols_in,
    local_sem, halo_send, halo_recv, a2a_send, a2a_recv, row_send, row_recv, col_send, col_recv,
):
    snaps, _, nx, ny, nz = vel_ref.shape
    total = snaps * n_snap
    half = snaps * ny // 2
    rows = snaps * ny
    part = rows // n_snap
    y_part = ny // n_snap
    pairs = nx // 2
    tile_rows = total // n_space
    chunks = 3 * pairs
    si = lax.axis_index("space")
    ti = lax.axis_index("snap")

    load_vw = pltpu.make_async_copy(vel_ref.at[:, 1:3], ext.at[:, :, 2 : nx + 2], local_sem.at[0])
    load_u = pltpu.make_async_copy(vel_ref.at[:, 0], uu, local_sem.at[1])
    load_bins = pltpu.make_async_copy(bins_hbm, bins_ref, local_sem.at[2])
    load_owner = pltpu.make_async_copy(owner_hbm, owner_ref, local_sem.at[3])
    load_vw.start()
    load_u.start()
    load_bins.start()
    load_owner.start()

    barrier = pltpu.get_barrier_semaphore()
    for o in range(1, n_snap):
        pl.semaphore_signal(
            barrier, inc=1, device_id={"snap": lax.rem(ti + o, n_snap)}, device_id_type=MESH
        )
    for o in range(1, n_space):
        pl.semaphore_signal(
            barrier, inc=1, device_id={"space": lax.rem(si + o, n_space)}, device_id_type=MESH
        )

    c = iota2((1, rows), 1)
    moved_to = (c % ny) * snaps + c // ny
    perm[...] = jnp.where(iota2((rows, rows), 0) == moved_to, 1.0, 0.0).astype(BF16)

    def band(size, length):
        r = iota2((size, size), 0)
        c = iota2((size, size), 1)
        first = (iota2((1, size), 1) // length) * length
        return jnp.where((r >= first) & (r < first + length), stencil(r - c), 0.0)

    band_y[...] = (-band(half, ny)).astype(BF16)
    band_z[...] = band(2 * nz, nz).astype(BF16)
    gram[...] = jnp.zeros_like(gram)

    def to_left(comp):
        return pltpu.make_async_remote_copy(
            vel_ref.at[:, comp + 1, 0:2], ext.at[:, comp, nx + 2 : nx + 4],
            halo_send.at[0, comp], halo_recv.at[0, comp],
            device_id={"space": si - 1}, device_id_type=MESH,
        )

    def to_right(comp):
        return pltpu.make_async_remote_copy(
            vel_ref.at[:, comp + 1, nx - 2 : nx], ext.at[:, comp, 0:2],
            halo_send.at[1, comp], halo_recv.at[1, comp],
            device_id={"space": si + 1}, device_id_type=MESH,
        )

    @pl.when(si == 0)
    def _():
        ext[:, :, 0:2] = jnp.zeros((snaps, 2, 2, ny, nz), BF16)

    @pl.when(si == n_space - 1)
    def _():
        ext[:, :, nx + 2 : nx + 4] = jnp.zeros((snaps, 2, 2, ny, nz), BF16)

    order = sorted(range(1, n_snap), key=lambda o: abs(o - n_snap // 2))

    def a2a(k, o):
        dst = lax.rem(ti + o, n_snap)
        return pltpu.make_async_remote_copy(
            send.at[k, pl.ds(pl.multiple_of(dst * part, part), part)],
            recv.at[k, ti],
            a2a_send.at[k, o - 1], a2a_recv.at[k, o - 1],
            device_id={"snap": dst}, device_id_type=MESH,
        )

    def arrange(k):
        moved = jnp.dot(perm[...], omega[...], preferred_element_type=F32)
        send[k] = moved.astype(BF16)

    def ship(k):
        for o in order:
            a2a(k, o).start()
        recv[k, ti] = send[k, pl.ds(pl.multiple_of(ti * part, part), part)]

    h_snaps = snaps // 2

    def pair_vw(comp, x, h):
        s = slice(h * h_snaps, (h + 1) * h_snaps)
        return jnp.concatenate(
            [ext[s, comp, x + 2 + i].reshape(half, nz) for i in range(2)], axis=1
        )

    def pair_u(x, h):
        s = slice(h * h_snaps, (h + 1) * h_snaps)
        return jnp.concatenate([uu[s, x + i].reshape(half, nz) for i in range(2)], axis=1)

    def d1_pair(comp, x, h):
        s = slice(h * h_snaps, (h + 1) * h_snaps)
        f = [ext[s, comp, x + i].reshape(half, nz).astype(F32) for i in range(6)]
        return jnp.concatenate(
            [8.0 * (f[i + 3] - f[i + 1]) - (f[i + 4] - f[i]) for i in range(2)], axis=1
        )

    def d2(field):
        return jnp.dot(band_y[...], field, preferred_element_type=F32)

    def d3(field):
        return jnp.dot(field, band_z[...], preferred_element_type=F32)

    def put(h, value):
        omega[h * half : (h + 1) * half] = (value * (1.0 / 12.0)).astype(BF16)

    def make_x(k, x):
        for h in range(2):
            put(h, d2(pair_vw(1, x, h)) - d3(pair_vw(0, x, h)))
        arrange(k)

    def make_y(k, x):
        for h in range(2):
            put(h, d3(pair_u(x, h)) - d1_pair(1, x, h))
        arrange(k)

    def make_z(k, x):
        for h in range(2):
            put(h, d1_pair(0, x, h) - d2(pair_u(x, h)))
        arrange(k)

    load_vw.wait()
    make_x(0, 0)

    pl.semaphore_wait(barrier, n_snap + n_space - 2)
    for comp in (1, 0):
        @pl.when(si > 0)
        def _():
            to_left(comp).start()

        @pl.when(si < n_space - 1)
        def _():
            to_right(comp).start()

    ship(0)

    def x_step(p, _):
        make_x(p, 2 * p)
        ship(p)
        return 0

    lax.fori_loop(1, pairs, x_step, 0)
    load_u.wait()

    def inner(p, _):
        k = pairs + 2 * p
        make_y(k, 2 * p + 2)
        ship(k)
        make_z(k + 1, 2 * p + 2)
        ship(k + 1)
        return 0

    lax.fori_loop(0, pairs - 2, inner, 0)

    load_bins.wait()
    load_owner.wait()
    onehot = jnp.where(bins_ref[...] == iota2((32, total), 0), 1.0, 0.0).astype(F32)
    same = lax.dot_general(
        onehot, onehot, (((0,), (0,)), ((), ())), preferred_element_type=F32
    )
    averaging = same / jnp.sum(same, axis=0, keepdims=True)
    mean_mat[...] = averaging.astype(BF16)
    r = iota2((total, total), 0)
    c = iota2((total, total), 1)
    centre = jnp.where(r == c, 1.0, 0.0) - averaging
    centre_mat[...] = centre
    c1 = iota2((1, total), 1)
    tile = c1 // tile_rows
    first_row = jnp.zeros((1, total), jnp.int32)
    for t in range(n_space):
        first_row = jnp.where(tile == t, owner_ref[t] * tile_rows, first_row)
    place = jnp.where(r == first_row + c1 % tile_rows, inv_voxels, 0.0)
    left_mat[...] = jnp.dot(place, centre, preferred_element_type=F32, precision=HIGH)

    def accumulate(k, _):
        for o in order:
            a2a(k, o).wait_recv()
        columns = jnp.concatenate(
            [
                jnp.concatenate(
                    [recv[k, t, y * snaps : (y + 1) * snaps] for t in range(n_snap)], axis=0
                )
                for y in range(y_part)
            ],
            axis=1,
        )
        mean = jnp.dot(mean_mat[...], columns, preferred_element_type=F32)
        near = (columns.astype(F32) - mean).astype(BF16)
        gram[...] += lax.dot_general(
            near, near, (((1,), (1,)), ((), ())), preferred_element_type=F32
        )
        return 0

    def edges(comp, make, base):
        @pl.when(si < n_space - 1)
        def _():
            to_left(comp).wait_recv()

        @pl.when(si > 0)
        def _():
            to_right(comp).wait_recv()

        def side(p, _):
            make(base + p, p * (nx - 2))
            ship(base + p)
            return 0

        lax.fori_loop(0, 2, side, 0)

    lax.fori_loop(0, 2, accumulate, 0)
    edges(1, make_y, chunks - 4)
    lax.fori_loop(2, 4, accumulate, 0)
    edges(0, make_z, chunks - 2)
    lax.fori_loop(4, chunks, accumulate, 0)

    lines = jnp.dot(left_mat[...], gram[...], preferred_element_type=F32, precision=HIGH)
    done = jnp.dot(lines, centre_mat[...], preferred_element_type=F32, precision=HIGH)
    mail[...] = jnp.zeros_like(mail)
    mail[:, 0:total] = done

    def row_copy(o):
        dst = lax.rem(si + o, n_space)
        return pltpu.make_async_remote_copy(
            mail.at[pl.ds(pl.multiple_of(dst * tile_rows, tile_rows), tile_rows)],
            rows_in.at[si], row_send.at[o - 1], row_recv.at[o - 1],
            device_id={"space": dst}, device_id_type=MESH,
        )

    for o in range(1, n_space):
        row_copy(o).start()
    rows_in[si] = mail[pl.ds(pl.multiple_of(si * tile_rows, tile_rows), tile_rows)]
    for o in range(1, n_space):
        row_copy(o).wait_recv()
    mine = jnp.sum(rows_in[...], axis=0)
    cols_out[...] = mine

    def col_copy(o):
        return pltpu.make_async_remote_copy(
            cols_out, cols_in.at[o - 1], col_send.at[o - 1], col_recv.at[o - 1],
            device_id={"snap": lax.rem(ti + o, n_snap)}, device_id_type=MESH,
        )

    for o in order:
        col_copy(o).start()
    for o in order:
        col_copy(o).wait_recv()
    out_ref[...] = mine + jnp.sum(cols_in[...], axis=0)

    def drain(k, _):
        for o in order:
            a2a(k, o).wait_send()
        return 0

    lax.fori_loop(0, chunks, drain, 0)

    for comp in range(2):
        @pl.when(si > 0)
        def _():
            to_left(comp).wait_send()

        @pl.when(si < n_space - 1)
        def _():
            to_right(comp).wait_send()

    for o in range(1, n_space):
        row_copy(o).wait_send()
    for o in order:
        col_copy(o).wait_send()


def per_device(velocity, phase_bins, tile_owner):
    n_space = lax.axis_size("space")
    n_snap = lax.axis_size("snap")
    snaps, _, nx, ny, nz = velocity.shape
    total = snaps * n_snap
    rows = snaps * ny
    part = rows // n_snap
    chunks = 3 * (nx // 2)
    tile_rows = total // n_space
    wide = -(-total // 128) * 128
    dma = pltpu.SemaphoreType.DMA
    summed = pl.pallas_call(
        functools.partial(kernel, n_space, n_snap, 1.0 / (n_space * nx * ny * nz)),
        out_shape=jax.ShapeDtypeStruct((tile_rows, wide), F32),
        in_specs=[
            pl.BlockSpec(memory_space=pl.ANY),
            pl.BlockSpec(memory_space=pl.ANY),
            pl.BlockSpec(memory_space=pl.ANY),
        ],
        out_specs=pl.BlockSpec(memory_space=pltpu.VMEM),
        scratch_shapes=[
            pltpu.SMEM((n_space,), jnp.int32),
            pltpu.VMEM((1, total), jnp.int32),
            pltpu.VMEM((snaps, 2, nx + 4, ny, nz), BF16),
            pltpu.VMEM((snaps, nx, ny, nz), BF16),
            pltpu.VMEM((rows, rows), BF16),
            pltpu.VMEM((rows // 2, rows // 2), BF16),
            pltpu.VMEM((2 * nz, 2 * nz), BF16),
            pltpu.VMEM((rows, 2 * nz), BF16),
            pltpu.VMEM((chunks, rows, 2 * nz), BF16),
            pltpu.VMEM((chunks, n_snap, part, 2 * nz), BF16),
            pltpu.VMEM((total, total), BF16),
            pltpu.VMEM((total, total), F32),
            pltpu.VMEM((total, total), F32),
            pltpu.VMEM((total, total), F32),
            pltpu.VMEM((total, wide), F32),
            pltpu.VMEM((n_space, tile_rows, wide), F32),
            pltpu.VMEM((tile_rows, wide), F32),
            pltpu.VMEM((n_snap - 1, tile_rows, wide), F32),
            dma((4,)),
            dma((2, 2)),
            dma((2, 2)),
            dma((chunks, n_snap - 1)),
            dma((chunks, n_snap - 1)),
            dma((n_space - 1,)),
            dma((n_space - 1,)),
            dma((n_snap - 1,)),
            dma((n_snap - 1,)),
        ],
        compiler_params=pltpu.CompilerParams(
            collective_id=0, has_side_effects=True, vmem_limit_bytes=62 * 1024 * 1024
        ),
        cost_estimate=pl.CostEstimate(
            flops=4_000_000_000, bytes_accessed=4_000_000, transcendentals=0
        ),
    )(tile_owner, phase_bins.reshape(1, total), velocity)
    return lax.dynamic_slice_in_dim(summed, lax.axis_index("snap") * snaps, snaps, axis=1)[None]


def solution(mesh):
    return jax.shard_map(
        per_device,
        mesh=mesh,
        in_specs=(P("snap", None, "space", None, None), P(), P()),
        out_specs=P("space", None, "snap"),
        check_vma=False,
    )
```

time: 55.7 us -> 51 us (0.916)
  local copies, waits for them, and re-layouts: 3.87 us -> 1.35 us
  Pallas kernels: 51.6 us -> 49.4 us
    unnamed x6 -> x0, local copies, waits for them, and re-layouts: 3.2 us -> none
    pallas_call x1, Pallas kernels: 51.6 us -> 49.4 us  [per_device(): pl.pallas_call(functools.partial(kernel, n_space, n_snap, 1.0 / (n_space...]
    broadcast_in_dim x1, local copies, waits for them, and re-layouts: 0.67 us -> 1.35 us  [per_device(): lax.dynamic_slice_in_dim(summed, lax.axis_index('snap') * snaps, snaps, a...]
where the time goes in v1:
time: 51 us; the launch traced here: 50.8 us
  Pallas kernels  49.4 us (97%)
  local copies, waits for them, and re-layouts  1.35 us (3%)
    pallas_call x1, Pallas kernels, per_device(): pl.pallas_call(functools.partial(kernel, n_space, n_snap, 1.0 / (n_space...  49.4 us
    broadcast_in_dim x1, local copies, waits for them, and re-layouts, per_device(): lax.dynamic_slice_in_dim(summed, lax.axis_index('snap') * snaps, snaps, a...  1.35 us

profile of v1, /device:TPU:0, one launch (start us, length us, event | category | flops | bytes accessed | tf_op | source)
XLA Modules:
  0.0 50.8 jit_solution(14976293454559235943)
XLA Ops:
  0.0 49.4 %shard_map.37 = f32[8,128]{1,0:T(8,128)} custom-call(s32[8]{0:T(128)} %owner_hbm.1, s32[1,64]{1,0:T(1,128)} %bitcast.3, bf16[16,3,8,32,128]{4,3,2,1,0:T(8,128)(2,1)} %vel_ref.1), custom_call_target="tpu_custom_call" | custom-call | flops 4000000000 | bytes 4000000 | tf_op jit(solution)/shard_map/pallas_call | solution.py:322
  49.5 1.4 %dynamic-slice_bitcast_fusion = f32[1,8,16]{2,1,0:T(8,128)} fusion(f32[8,128]{1,0:T(8,128)} %shard_map.37, s32[]{:T(128)S(6)} %select_n.3), kind=kLoop, calls=%fused_computation | loop fusion | bytes 1028 | tf_op jit(solution)/shard_map/broadcast_in_dim | solution.py:367

commit v2 on v1

--- a/solution.py
+++ b/solution.py
@@ -26,7 +26,7 @@
 def kernel(
     n_space, n_snap, inv_voxels,
     owner_hbm, bins_hbm, vel_ref, out_ref,
-    owner_ref, bins_ref, ext, uu, perm, band_y, band_z, omega, send, recv, mean_mat, centre_mat, left_mat, gram, mail, rows_in, cols_out, cols_in,
+    owner_ref, bins_ref, ext, uu, perm, band_y, band_z, omega, send, recv, weights, mail, rows_in, cols_out, cols_in,
     local_sem, halo_send, halo_recv, a2a_send, a2a_recv, row_send, row_recv, col_send, col_recv,
 ):
     snaps, _, nx, ny, nz = vel_ref.shape
@@ -72,7 +72,7 @@
 
     band_y[...] = (-band(half, ny)).astype(BF16)
     band_z[...] = band(2 * nz, nz).astype(BF16)
-    gram[...] = jnp.zeros_like(gram)
+    mail[...] = jnp.zeros_like(mail)
 
     def to_left(comp):
         return pltpu.make_async_remote_copy(
@@ -199,18 +199,24 @@
         onehot, onehot, (((0,), (0,)), ((), ())), preferred_element_type=F32
     )
     averaging = same / jnp.sum(same, axis=0, keepdims=True)
-    mean_mat[...] = averaging.astype(BF16)
     r = iota2((total, total), 0)
     c = iota2((total, total), 1)
     centre = jnp.where(r == c, 1.0, 0.0) - averaging
-    centre_mat[...] = centre
     c1 = iota2((1, total), 1)
     tile = c1 // tile_rows
     first_row = jnp.zeros((1, total), jnp.int32)
     for t in range(n_space):
         first_row = jnp.where(tile == t, owner_ref[t] * tile_rows, first_row)
-    place = jnp.where(r == first_row + c1 % tile_rows, inv_voxels, 0.0)
-    left_mat[...] = jnp.dot(place, centre, preferred_element_type=F32, precision=HIGH)
+    place = jnp.where(r == first_row + c1 % tile_rows, 1.0, 0.0)
+    rest = jnp.concatenate(
+        [centre, jnp.dot(place, centre, preferred_element_type=F32, precision=HIGH)], axis=0
+    )
+    pieces = []
+    for term in range(3):
+        piece = rest.astype(BF16).astype(F32)
+        pieces.append(piece)
+        rest = rest - piece
+    weights[...] = jnp.concatenate(pieces, axis=1).astype(BF16)
 
     def accumulate(k, _):
         for o in order:
@@ -224,10 +230,11 @@
             ],
             axis=1,
         )
-        mean = jnp.dot(mean_mat[...], columns, preferred_element_type=F32)
-        near = (columns.astype(F32) - mean).astype(BF16)
-        gram[...] += lax.dot_general(
-            near, near, (((1,), (1,)), ((), ())), preferred_element_type=F32
+        near = jnp.dot(
+            weights[...], jnp.concatenate([columns] * 3, axis=0), preferred_element_type=F32
+        ).astype(BF16)
+        mail[:, 0:total] += lax.dot_general(
+            near[total:], near[:total], (((1,), (1,)), ((), ())), preferred_element_type=F32
         )
         return 0
 
@@ -253,11 +260,6 @@
     edges(0, make_z, chunks - 2)
     lax.fori_loop(4, chunks, accumulate, 0)
 
-    lines = jnp.dot(left_mat[...], gram[...], preferred_element_type=F32, precision=HIGH)
-    done = jnp.dot(lines, centre_mat[...], preferred_element_type=F32, precision=HIGH)
-    mail[...] = jnp.zeros_like(mail)
-    mail[:, 0:total] = done
-
     def row_copy(o):
         dst = lax.rem(si + o, n_space)
         return pltpu.make_async_remote_copy(
@@ -266,12 +268,12 @@
             device_id={"space": dst}, device_id_type=MESH,
         )
 
-    for o in range(1, n_space):
+    for o in sorted(range(1, n_space), key=lambda o: abs(o - n_space // 2)):
         row_copy(o).start()
     rows_in[si] = mail[pl.ds(pl.multiple_of(si * tile_rows, tile_rows), tile_rows)]
     for o in range(1, n_space):
         row_copy(o).wait_recv()
-    mine = jnp.sum(rows_in[...], axis=0)
+    mine = jnp.sum(rows_in[...], axis=0) * inv_voxels
     cols_out[...] = mine
 
     def col_copy(o):
@@ -284,7 +286,10 @@
         col_copy(o).start()
     for o in order:
         col_copy(o).wait_recv()
-    out_ref[...] = mine + jnp.sum(cols_in[...], axis=0)
+    summed = mine + jnp.sum(cols_in[...], axis=0)
+    wide = summed.shape[1]
+    turned = pltpu.roll(summed, lax.rem(wide - ti * snaps, wide), 1)
+    out_ref[0] = turned[:, 0:snaps]
 
     def drain(k, _):
         for o in order:
@@ -319,9 +324,9 @@
     tile_rows = total // n_space
     wide = -(-total // 128) * 128
     dma = pltpu.SemaphoreType.DMA
-    summed = pl.pallas_call(
+    return pl.pallas_call(
         functools.partial(kernel, n_space, n_snap, 1.0 / (n_space * nx * ny * nz)),
-        out_shape=jax.ShapeDtypeStruct((tile_rows, wide), F32),
+        out_shape=jax.ShapeDtypeStruct((1, tile_rows, snaps), F32),
         in_specs=[
             pl.BlockSpec(memory_space=pl.ANY),
             pl.BlockSpec(memory_space=pl.ANY),
@@ -339,10 +344,7 @@
             pltpu.VMEM((rows, 2 * nz), BF16),
             pltpu.VMEM((chunks, rows, 2 * nz), BF16),
             pltpu.VMEM((chunks, n_snap, part, 2 * nz), BF16),
-            pltpu.VMEM((total, total), BF16),
-            pltpu.VMEM((total, total), F32),
-            pltpu.VMEM((total, total), F32),
-            pltpu.VMEM((total, total), F32),
+            pltpu.VMEM((2 * total, 3 * total), BF16),
             pltpu.VMEM((total, wide), F32),
             pltpu.VMEM((n_space, tile_rows, wide), F32),
             pltpu.VMEM((tile_rows, wide), F32),
@@ -364,7 +366,6 @@
             flops=4_000_000_000, bytes_accessed=4_000_000, transcendentals=0
         ),
     )(tile_owner, phase_bins.reshape(1, total), velocity)
-    return lax.dynamic_slice_in_dim(summed, lax.axis_index("snap") * snaps, snaps, axis=1)[None]
 
 
 def solution(mesh):

time: 51 us -> 51 us (level)
    broadcast_in_dim x1 -> x0, local copies, waits for them, and re-layouts: 1.35 us -> none  [per_device(): lax.dynamic_slice_in_dim(summed, lax.axis_index('snap') * snaps, snaps, a...]
    unnamed x0 -> x1, local copies, waits for them, and re-layouts: none -> 1.28 us
where the time goes in v2:
time: 51 us; the launch traced here: 50.8 us
  Pallas kernels  49.5 us (97%)
  local copies, waits for them, and re-layouts  1.28 us (3%)
    pallas_call x1, Pallas kernels, per_device(): pl.pallas_call(functools.partial(kernel, n_space, n_snap, 1.0 / (n_space...  49.5 us
    unnamed x1, local copies, waits for them, and re-layouts  1.28 us

profile of v2, /device:TPU:0, one launch (start us, length us, event | category | flops | bytes accessed | tf_op | source)
XLA Modules:
  0.0 50.8 jit_solution(8857630738500161244)
XLA Ops:
  0.0 49.5 %shard_map.37 = f32[1,8,16]{2,1,0:T(8,128)} custom-call(s32[8]{0:T(128)} %owner_hbm.1, s32[1,64]{1,0:T(1,128)} %bitcast.1, bf16[16,3,8,32,128]{4,3,2,1,0:T(8,128)(2,1)} %vel_ref.1), custom_call_target="tpu_custom_call" | custom-call | flops 4000000000 | bytes 4000000 | tf_op jit(solution)/shard_map/pallas_call | solution.py:327
  49.5 1.3 %copy.5 = f32[1,8,16]{2,1,0:T(8,128)} copy(f32[1,8,16]{2,1,0:T(8,128)} %shard_map.37) | data formatting | bytes 1024

commit v3 on v2

--- a/solution.py
+++ b/solution.py
@@ -26,7 +26,7 @@
 def kernel(
     n_space, n_snap, inv_voxels,
     owner_hbm, bins_hbm, vel_ref, out_ref,
-    owner_ref, bins_ref, ext, uu, perm, band_y, band_z, omega, send, recv, weights, mail, rows_in, cols_out, cols_in,
+    owner_ref, bins_ref, ext, uu, perm, band_y, band_z, omega, send, recv, terms, weights, mail, rows_in, cols_out, cols_in,
     local_sem, halo_send, halo_recv, a2a_send, a2a_recv, row_send, row_recv, col_send, col_recv,
 ):
     snaps, _, nx, ny, nz = vel_ref.shape
@@ -163,7 +163,9 @@
     make_x(0, 0)
 
     pl.semaphore_wait(barrier, n_snap + n_space - 2)
-    for comp in (1, 0):
+    ship(0)
+
+    def start_halo(comp):
         @pl.when(si > 0)
         def _():
             to_left(comp).start()
@@ -172,7 +174,7 @@
         def _():
             to_right(comp).start()
 
-    ship(0)
+    start_halo(1)
 
     def x_step(p, _):
         make_x(p, 2 * p)
@@ -180,6 +182,7 @@
         return 0
 
     lax.fori_loop(1, pairs, x_step, 0)
+    start_halo(0)
     load_u.wait()
 
     def inner(p, _):
@@ -211,12 +214,12 @@
     rest = jnp.concatenate(
         [centre, jnp.dot(place, centre, preferred_element_type=F32, precision=HIGH)], axis=0
     )
-    pieces = []
     for term in range(3):
-        piece = rest.astype(BF16).astype(F32)
-        pieces.append(piece)
-        rest = rest - piece
-    weights[...] = jnp.concatenate(pieces, axis=1).astype(BF16)
+        terms[term] = rest.astype(BF16)
+        rest = rest - terms[term].astype(F32)
+    weights[...] = jnp.concatenate(
+        [terms[term].astype(F32) for term in range(3)], axis=1
+    ).astype(BF16)
 
     def accumulate(k, _):
         for o in order:
@@ -328,9 +331,9 @@
         functools.partial(kernel, n_space, n_snap, 1.0 / (n_space * nx * ny * nz)),
         out_shape=jax.ShapeDtypeStruct((1, tile_rows, snaps), F32),
         in_specs=[
-            pl.BlockSpec(memory_space=pl.ANY),
-            pl.BlockSpec(memory_space=pl.ANY),
-            pl.BlockSpec(memory_space=pl.ANY),
+            pl.BlockSpec(memory_space=pltpu.HBM),
+            pl.BlockSpec(memory_space=pltpu.HBM),
+            pl.BlockSpec(memory_space=pltpu.HBM),
         ],
         out_specs=pl.BlockSpec(memory_space=pltpu.VMEM),
         scratch_shapes=[
@@ -344,6 +347,7 @@
             pltpu.VMEM((rows, 2 * nz), BF16),
             pltpu.VMEM((chunks, rows, 2 * nz), BF16),
             pltpu.VMEM((chunks, n_snap, part, 2 * nz), BF16),
+            pltpu.VMEM((3, 2 * total, total), BF16),
             pltpu.VMEM((2 * total, 3 * total), BF16),
             pltpu.VMEM((total, wide), F32),
             pltpu.VMEM((n_space, tile_rows, wide), F32),
@@ -360,7 +364,7 @@
             dma((n_snap - 1,)),
         ],
         compiler_params=pltpu.CompilerParams(
-            collective_id=0, has_side_effects=True, vmem_limit_bytes=62 * 1024 * 1024
+            collective_id=0, has_side_effects=True, vmem_limit_bytes=61952 * 1024
         ),
         cost_estimate=pl.CostEstimate(
             flops=4_000_000_000, bytes_accessed=4_000_000, transcendentals=0

time: 51 us -> 50.9 us (level)
  no operation moved by 1% of the time
where the time goes in v3:
time: 50.9 us; the launch traced here: 50.8 us
  Pallas kernels  49.5 us (97%)
  local copies, waits for them, and re-layouts  1.28 us (3%)
    pallas_call x1, Pallas kernels, per_device(): pl.pallas_call(functools.partial(kernel, n_space, n_snap, 1.0 / (n_space...  49.5 us
    unnamed x1, local copies, waits for them, and re-layouts  1.28 us

profile of v3, /device:TPU:0, one launch (start us, length us, event | category | flops | bytes accessed | tf_op | source)
XLA Modules:
  0.0 50.8 jit_solution(8901485228875781627)
XLA Ops:
  0.0 49.5 %shard_map.37 = f32[1,8,16]{2,1,0:T(8,128)} custom-call(s32[8]{0:T(128)} %owner_hbm.1, s32[1,64]{1,0:T(1,128)} %bitcast.1, bf16[16,3,8,32,128]{4,3,2,1,0:T(8,128)(2,1)} %vel_ref.1), custom_call_target="tpu_custom_call" | custom-call | flops 4000000000 | bytes 4000000 | tf_op jit(solution)/shard_map/pallas_call | solution.py:330
  49.5 1.3 %copy.5 = f32[1,8,16]{2,1,0:T(8,128)} copy(f32[1,8,16]{2,1,0:T(8,128)} %shard_map.37) | data formatting | bytes 1024

commit v4 on v1

--- a/solution.py
+++ b/solution.py
@@ -41,7 +41,11 @@
     si = lax.axis_index("space")
     ti = lax.axis_index("snap")
 
-    load_vw = pltpu.make_async_copy(vel_ref.at[:, 1:3], ext.at[:, :, 2 : nx + 2], local_sem.at[0])
+    load_first = pltpu.make_async_copy(vel_ref.at[:, 1:3, 0:2], ext.at[:, :, 2:4], local_sem.at[4])
+    load_vw = pltpu.make_async_copy(
+        vel_ref.at[:, 1:3, 2:nx], ext.at[:, :, 4 : nx + 2], local_sem.at[0]
+    )
+    load_first.start()
     load_u = pltpu.make_async_copy(vel_ref.at[:, 0], uu, local_sem.at[1])
     load_bins = pltpu.make_async_copy(bins_hbm, bins_ref, local_sem.at[2])
     load_owner = pltpu.make_async_copy(owner_hbm, owner_ref, local_sem.at[3])
@@ -159,10 +163,11 @@
             put(h, d1_pair(0, x, h) - d2(pair_u(x, h)))
         arrange(k)
 
-    load_vw.wait()
+    load_first.wait()
     make_x(0, 0)
 
     pl.semaphore_wait(barrier, n_snap + n_space - 2)
+    ship(0)
     for comp in (1, 0):
         @pl.when(si > 0)
         def _():
@@ -172,7 +177,7 @@
         def _():
             to_right(comp).start()
 
-    ship(0)
+    load_vw.wait()
 
     def x_step(p, _):
         make_x(p, 2 * p)
@@ -347,7 +352,7 @@
             pltpu.VMEM((n_space, tile_rows, wide), F32),
             pltpu.VMEM((tile_rows, wide), F32),
             pltpu.VMEM((n_snap - 1, tile_rows, wide), F32),
-            dma((4,)),
+            dma((5,)),
             dma((2, 2)),
             dma((2, 2)),
             dma((chunks, n_snap - 1)),

time: 51 us -> 50.7 us (level)
  no operation moved by 1% of the time
where the time goes in v4:
time: 50.7 us; the launch traced here: 50.6 us
  Pallas kernels  49.2 us (97%)
  local copies, waits for them, and re-layouts  1.35 us (3%)
    pallas_call x1, Pallas kernels, per_device(): pl.pallas_call(functools.partial(kernel, n_space, n_snap, 1.0 / (n_space...  49.2 us
    broadcast_in_dim x1, local copies, waits for them, and re-layouts, per_device(): lax.dynamic_slice_in_dim(summed, lax.axis_index('snap') * snaps, snaps, a...  1.35 us

profile of v4, /device:TPU:0, one launch (start us, length us, event | category | flops | bytes accessed | tf_op | source)
XLA Modules:
  0.0 50.6 jit_solution(3669362725899526997)
XLA Ops:
  0.0 49.2 %shard_map.37 = f32[8,128]{1,0:T(8,128)} custom-call(s32[8]{0:T(128)} %owner_hbm.1, s32[1,64]{1,0:T(1,128)} %bitcast.3, bf16[16,3,8,32,128]{4,3,2,1,0:T(8,128)(2,1)} %vel_ref.1), custom_call_target="tpu_custom_call" | custom-call | flops 4000000000 | bytes 4000000 | tf_op jit(solution)/shard_map/pallas_call | solution.py:327
  49.2 1.4 %dynamic-slice_bitcast_fusion = f32[1,8,16]{2,1,0:T(8,128)} fusion(f32[8,128]{1,0:T(8,128)} %shard_map.37, s32[]{:T(128)S(6)} %select_n.3), kind=kLoop, calls=%fused_computation | loop fusion | bytes 1028 | tf_op jit(solution)/shard_map/broadcast_in_dim | solution.py:372
